TPU v7x, 32 devices: a whole 2x2x4 slice. The times are simulated.
32 devices in a mesh: blk: 4 (over y, core), group: 8 (over z, x).
Axes of the slice: x: 2, y: 2, z: 4, core: 2. Of those that a mesh axis runs over, the one named last changes fastest.
Arguments:
- student_features: bfloat16 [4096, 768], P(('blk', 'group')), may hold values from -8 to 8
- teacher_image: bfloat16 [4096, 1152], P(('blk', 'group')), may hold values from -8 to 8
- text_embeds: bfloat16 [4096, 1152], P(('blk', 'group')), may hold values from -8 to 8
- pair_ids: int32 [4096], replicated, may hold values from 0 to 511
- head_weights: bfloat16 [1152, 768], replicated, may hold values from -1 to 1
- moment_first: float32 [1152, 768], P('group'), may hold values from -4 to 4
- moment_second: float32 [1152, 768], P('group'), may hold values from 0.01 to 0.3
Outputs:
- row_loss: float32 [4096], P(('blk', 'group'))
- new_first: float32 [1152, 768], P('group')
- new_second: float32 [1152, 768], P('group')
- new_weights: bfloat16 [1152, 768], replicated
All inputs are finite; a program needn't handle non-finite values.
Results may differ from a plain program's by a relative error of at most 0.0025.
The roundings to bfloat16 on the way count: a program that leaves them out, or rounds other values in their place, can miss the bound.
Values may be sent and summed in bfloat16 or wider, within the bound.
A program may use at most 64 MiB of HBM per device.

v0:
```python
import jax
import jax.numpy as jnp
from jax import lax
from jax.sharding import PartitionSpec as P

student_scale = 20.0
student_bias = -1.0
teacher_scale = 25.0
teacher_bias = -1.5
label_mix = 0.5
norm_eps = 1e-06
beta_one = 0.9
beta_two = 0.95
learn_rate = 0.01
weight_decay = 0.0001
adam_eps = 1e-08
adam_step = 100.0


def from_partner(shard, axis, bit):
    return lax.ppermute(shard, axis, [(i, i ^ 1 << bit) for i in range(lax.axis_size(axis))])


def unit_rows(values):
    values = values.astype(jnp.float32)
    return values * lax.rsqrt(jnp.sum(values * values, axis=-1, keepdims=True) + norm_eps)


def pair_terms(student_rows, teacher_rows, left_ids, text_rows, right_ids):
    dims = (((1,), (1,)), ((), ()))
    student_logit = (
        student_scale
        * lax.dot_general(student_rows, text_rows, dims, preferred_element_type=jnp.float32)
        + student_bias
    )
    teacher_logit = (
        teacher_scale
        * lax.dot_general(teacher_rows, text_rows, dims, preferred_element_type=jnp.float32)
        + teacher_bias
    )
    labels = (left_ids[:, None] == right_ids[None, :]).astype(jnp.float32)
    target = (1.0 - label_mix) * labels + label_mix * jax.nn.sigmoid(teacher_logit)
    losses = jnp.sum(jax.nn.softplus(student_logit) - target * student_logit, axis=1)
    coeff = (jax.nn.sigmoid(student_logit) - target).astype(jnp.bfloat16)
    pulled = jnp.dot(coeff, text_rows, preferred_element_type=jnp.float32)
    return (losses, pulled)


def per_device(
    student_features,
    teacher_image,
    text_embeds,
    pair_ids,
    head_weights,
    moment_first,
    moment_second,
):
    row_count = student_features.shape[0]
    blk_count = lax.axis_size("blk")
    group_count = lax.axis_size("group")
    swap_bit = group_count.bit_length() - 2
    group_index = lax.axis_index("group")
    partner_index = (group_index + group_count // 2) % group_count
    blk_index = lax.axis_index("blk")
    projected = lax.dot_general(
        student_features, head_weights, (((1,), (1,)), ((), ())), preferred_element_type=jnp.float32
    )
    inverse = lax.rsqrt(jnp.sum(projected * projected, axis=-1, keepdims=True) + norm_eps)
    student = projected * inverse
    student_b = student.astype(jnp.bfloat16)
    teacher_b = unit_rows(teacher_image).astype(jnp.bfloat16)
    texts_b = unit_rows(text_embeds).astype(jnp.bfloat16)
    ids_grid = pair_ids.reshape(blk_count, group_count, row_count)
    own_ids = lax.dynamic_index_in_dim(ids_grid, group_index, 1, keepdims=False)
    far_ids = lax.dynamic_index_in_dim(ids_grid, partner_index, 1, keepdims=False)
    left_ids = lax.dynamic_index_in_dim(own_ids, blk_index, 0, keepdims=False)
    far_block = from_partner(texts_b, "group", swap_bit)
    paired = jnp.concatenate([texts_b, far_block], axis=0)
    paired_ids = jnp.stack([own_ids, far_ids], axis=1).reshape(-1)
    losses, pulled = pair_terms(
        student_b,
        teacher_b,
        left_ids,
        lax.all_gather(paired, "blk", axis=0, tiled=True),
        paired_ids,
    )
    totals = (losses, pulled)
    losses, pulled = totals
    row_loss = losses / row_count
    grad_student = student_scale / row_count * pulled
    grad_projected = (
        inverse * (grad_student - student * jnp.sum(student * grad_student, axis=-1, keepdims=True))
    ).astype(jnp.bfloat16)
    shard_rows = moment_first.shape[0]
    group_grad = lax.psum_scatter(
        lax.dot_general(
            grad_projected,
            student_features,
            (((0,), (0,)), ((), ())),
            preferred_element_type=jnp.float32,
        ),
        "group",
        scatter_dimension=0,
        tiled=True,
    )
    head_grad = lax.psum(group_grad, "blk")
    new_first = beta_one * moment_first + (1.0 - beta_one) * head_grad
    new_second = beta_two * moment_second + (1.0 - beta_two) * head_grad * head_grad
    first_hat = new_first / (1.0 - beta_one**adam_step)
    second_hat = new_second / (1.0 - beta_two**adam_step)
    own_weights = lax.dynamic_slice_in_dim(
        head_weights, group_index * shard_rows, shard_rows, 0
    ).astype(jnp.float32)
    updated = own_weights - learn_rate * (
        first_hat / (jnp.sqrt(second_hat) + adam_eps) + weight_decay * own_weights
    )
    new_weights = lax.all_gather(updated.astype(jnp.bfloat16), "group", axis=0, tiled=True)
    return (row_loss, new_first, new_second, new_weights)


def solution(mesh):
    placed = (
        P(("blk", "group"), None),
        P(("blk", "group"), None),
        P(("blk", "group"), None),
        P(),
        P(),
        P("group", None),
        P("group", None),
    )
    return jax.shard_map(
        per_device,
        mesh=mesh,
        in_specs=placed,
        out_specs=(P(("blk", "group")), P("group", None), P("group", None), P()),
        check_vma=False,
    )
```

profile of v0, /device:TPU:0, one launch (start us, length us, event | category | flops | bytes accessed | tf_op | source)
XLA Modules:
  0.0 232.9 jit_solution(1380171829529624564)
XLA Ops:
  7.2 0.0 copy-start
  7.2 0.0 copy-start.4
  7.2 0.0 copy-start.1
  7.2 0.0 all-gather.3.cloned.1.call-start
  7.2 1.3 fusion.8
  8.5 1.1 fusion.9
  9.6 4.1 %collective-permute-start = (bf16[128,1152]{1,0:T(8,128)(2,1)S(1)}, bf16[128,1152]{1,0:T(8,128)(2,1)S(1)}, u32[]{:S(2)}, u32[]{:S(2)}) collective-permute-start(bf16[128,1152]{1,0:T(8,128)(2,1)S(1)} %fusion.9), channel_id=1, source_target_pairs={{0,4},{1,5},{2,6},{3,7},{4,0},{5,1},{6,2},{7,3},{8,12},{9,13},{10,... | collective-permute-start | bytes 884744 | tf_op jit(solution)/shard_map/ppermute | solution.py:21
  13.7 13.3 %collective-permute-done = bf16[128,1152]{1,0:T(8,128)(2,1)S(1)} collective-permute-done((bf16[128,1152]{1,0:T(8,128)(2,1)S(1)}, bf16[128,1152]{1,0:T(8,128)(2,1)S(1)}, u32[]{:S(2)}, u32[]{:S(2)}) %collective-permute-start) | collective-permute-done | bytes 294944 | tf_op jit(solution)/shard_map/ppermute | solution.py:21
  27.0 0.9 pad_maximum_fusion
  27.9 0.0 all-gather.3.cloned.1.call-update
  27.9 0.0 reduce-scatter.2.cloned.1.call-start
  28.0 0.7 fusion.25
  28.7 0.8 constant_dynamic-slice_fusion.1
  29.5 0.0 copy-done.4
  29.5 0.1 fusion.10
  29.6 0.0 copy-done
  29.7 0.0 copy-done.1
  29.7 0.8 multiply_reduce_fusion.1
  30.5 22.9 %all-gather.3.cloned.1.call-done = bf16[1024,1152]{1,0:T(8,128)(2,1)} async-done(((bf16[256,1152]{1,0:T(8,128)(2,1)}), bf16[1024,1152]{1,0:T(8,128)(2,1)}) %all-gather.3.cloned.1.call-update) | async-done | bytes 2359312 | tf_op jit(solution)/shard_map/all_gather | solution.py:84
  53.3 0.0 copy-start.5
  53.3 2.8 %fusion.6 = f32[128,1024]{1,0:T(8,128)S(1)} fusion(bf16[1024,1152]{1,0:T(8,128)(2,1)} %all-gather.3.cloned.1.call-done, bf16[128,1152]{1,0:T(8,128)(2,1)S(1)} %copy-done.4, f32[128]{0:T(128)S(1)} %add_rsqrt_fusion, s32[1024]{0:T(1024)S(1)} %bitcast.10, s32[128]{0:T(128)S(1)} %fusion.25), kind=kOutput, calls=%fused_computation.9 | convolution fusion | flops 303611904 | bytes 3183616 | tf_op jit(solution)/shard_map/dot_general | solution.py:38
  56.1 0.0 copy-done.5
  56.1 1.2 fusion.13
  57.3 0.7 multiply_reduce_fusion
  58.0 2.5 %fusion.18 = f32[1152,768]{1,0:T(8,128)} fusion(bf16[128,768]{1,0:T(8,128)(2,1)S(1)} %copy-done, f32[128,1152]{1,0:T(8,128)S(1)} %get-tuple-element.14, f32[128,1152]{1,0:T(8,128)S(1)} %get-tuple-element.10, f32[128]{0:T(128)S(1)} %get-tuple-element.13, f32[128]{0:T(128)S(1)} %add_rsqrt_fusion.2), kind=kOutput, calls=%fused_computation.36 | convolution fusion | flops 227229696 | bytes 4916224 | tf_op jit(solution)/shard_map/dot_general | solution.py:96
  60.5 0.0 copy-start.2
  60.5 0.0 copy-start.3
  60.5 0.0 reduce-scatter.2.cloned.1.call-update
  60.5 0.0 all-reduce.2.cloned.1.call-start
  60.5 79.3 %reduce-scatter.2.cloned.1.call-done = f32[144,768]{1,0:T(8,128)} async-done(((f32[1152,768]{1,0:T(8,128)}), f32[144,768]{1,0:T(8,128)}) %reduce-scatter.2.cloned.1.call-update) | async-done | bytes 442384 | tf_op jit(solution)/shard_map/reduce_scatter | solution.py:95
  139.9 0.0 all-reduce.2.cloned.1.call-update
  139.9 0.0 all-gather.5.cloned.1.call-start
  139.9 34.7 %all-reduce.2.cloned.1.call-done = f32[144,768]{1,0:T(8,128)} async-done(((f32[144,768]{1,0:T(8,128)}), f32[144,768]{1,0:T(8,128)}) %all-reduce.2.cloned.1.call-update) | async-done | bytes 442384 | tf_op jit(solution)/shard_map/psum | solution.py:106
  174.6 0.0 copy-done.2
  174.6 0.0 copy-done.3
  174.6 2.2 fusion.16
  176.8 0.0 all-gather.5.cloned.1.call-update
  176.8 0.5 broadcast_multiply_fusion
  177.4 46.3 %all-gather.5.cloned.1.call-done = bf16[1152,768]{1,0:T(8,128)(2,1)} async-done(((bf16[144,768]{1,0:T(8,128)(2,1)}), bf16[1152,768]{1,0:T(8,128)(2,1)}) %all-gather.5.cloned.1.call-update) | async-done | bytes 1769488 | tf_op jit(solution)/shard_map/all_gather | solution.py:117
  223.6 2.8 %copy.13 = bf16[1152,768]{1,0:T(8,128)(2,1)} copy(bf16[1152,768]{1,0:T(8,128)(2,1)} %all-gather.5.cloned.1.call-done) | data formatting | bytes 3538944
  (4 shorter events, 0.0 us)
Async XLA Ops:
  7.2 22.5 %copy-start = (bf16[128,768]{1,0:T(8,128)(2,1)S(1)}, bf16[128,768]{1,0:T(8,128)(2,1)}, u32[]{:S(2)}) copy-start(bf16[128,768]{1,0:T(8,128)(2,1)} %param.7) | copy-start | bytes 589828
  7.2 22.3 %copy-start.4 = (bf16[128,1152]{1,0:T(8,128)(2,1)S(1)}, bf16[128,1152]{1,0:T(8,128)(2,1)}, u32[]{:S(2)}) copy-start(bf16[128,1152]{1,0:T(8,128)(2,1)} %param.8) | copy-start | bytes 884740
  7.2 22.5 %copy-start.1 = (bf16[1152,768]{1,0:T(8,128)(2,1)S(1)}, bf16[1152,768]{1,0:T(8,128)(2,1)}, u32[]{:S(2)}) copy-start(bf16[1152,768]{1,0:T(8,128)(2,1)} %param.11) | copy-start | bytes 5308420
  7.2 46.1 %all-gather.3.cloned.1.call-start = ((), (), s32[]{:S(2)}) async-start(), calls=%async_computation.1 | async-start | bytes 2949120 | tf_op jit(solution)/shard_map/all_gather | solution.py:84
  9.6 17.4 %collective-permute-start = (bf16[128,1152]{1,0:T(8,128)(2,1)S(1)}, bf16[128,1152]{1,0:T(8,128)(2,1)S(1)}, u32[]{:S(2)}, u32[]{:S(2)}) collective-permute-start(bf16[128,1152]{1,0:T(8,128)(2,1)S(1)} %fusion.9), channel_id=1, source_target_pairs={{0,4},{1,5},{2,6},{3,7},{4,0},{5,1},{6,2},{7,3},{8,12},{9,13},{10,... | collective-permute-start | bytes 884744 | tf_op jit(solution)/shard_map/ppermute | solution.py:21
  27.9 111.9 %reduce-scatter.2.cloned.1.call-start = ((), (), s32[]{:S(2)}) async-start(), calls=%async_computation.2 | async-start | bytes 3981312 | tf_op jit(solution)/shard_map/reduce_scatter | solution.py:95
  53.3 2.8 %copy-start.5 = (bf16[1024,1152]{1,0:T(8,128)(2,1)S(1)}, bf16[1024,1152]{1,0:T(8,128)(2,1)}, u32[]{:S(2)}) copy-start(bf16[1024,1152]{1,0:T(8,128)(2,1)} %all-gather.3.cloned.1.call-done) | copy-start | bytes 7077892
  60.5 114.1 %copy-start.2 = (f32[144,768]{1,0:T(8,128)S(1)}, f32[144,768]{1,0:T(8,128)}, u32[]{:S(2)}) copy-start(f32[144,768]{1,0:T(8,128)} %param.13) | copy-start | bytes 1327108
  60.5 114.1 %copy-start.3 = (f32[144,768]{1,0:T(8,128)S(1)}, f32[144,768]{1,0:T(8,128)}, u32[]{:S(2)}) copy-start(f32[144,768]{1,0:T(8,128)} %param.12) | copy-start | bytes 1327108
  60.5 114.1 %all-reduce.2.cloned.1.call-start = ((), (), s32[]{:S(2)}) async-start(), calls=%async_computation.3 | async-start | bytes 884736 | tf_op jit(solution)/shard_map/psum | solution.py:106
  139.9 83.7 %all-gather.5.cloned.1.call-start = ((), (), s32[]{:S(2)}) async-start(), calls=%async_computation.4 | async-start | bytes 1990656 | tf_op jit(solution)/shard_map/all_gather | solution.py:117
Sparse Core Ops, SparseCore 0:
  28.0 25.2 all-gather.2
  60.6 79.2 reduce-scatter.1
  142.2 32.3 all-reduce.1
  177.4 46.1 all-gather.4
where the time goes:
time: 233 us
  waiting for transfers between devices  197 us (85%)
  between operations  13.9 us (6%)
  matrix products  7.89 us (3%)
  other arithmetic  6.1 us (3%)
  local copies, waits for them, and re-layouts  4.32 us (2%)
  starting transfers between devices  4.26 us (2%)
    reduce_scatter x1, waiting for transfers between devices, per_device(): lax.psum_scatter(lax.dot_general(grad_projected, student_features, (((0,)...  79.3 us
    all_gather x1, waiting for transfers between devices, per_device(): lax.all_gather(updated.astype(jnp.bfloat16), 'group', axis=0, tiled=True)  46.3 us
    psum x1, waiting for transfers between devices, per_device(): head_grad = lax.psum(group_grad, 'blk')  34.7 us
    all_gather x1, waiting for transfers between devices, per_device(): lax.all_gather(paired, 'blk', axis=0, tiled=True)  22.9 us
    ppermute x1, waiting for transfers between devices, from_partner(): lax.ppermute(shard, axis, [(i, i ^ 1 << bit) for i in range(lax.axis_size...  13.3 us
  transfers between devices with their start and end apart: 5, of which 5 were waited for; matrix products, arithmetic and copies ran while one was open for 1% of the time, Pallas kernels for 0%

commit v1 on v0

--- a/solution.py
+++ b/solution.py
@@ -1,6 +1,10 @@
+import functools
+
 import jax
 import jax.numpy as jnp
 from jax import lax
+from jax.experimental import pallas as pl
+from jax.experimental.pallas import tpu as pltpu
 from jax.sharding import PartitionSpec as P
 
 student_scale = 20.0
@@ -118,6 +122,372 @@
     return (row_loss, new_first, new_second, new_weights)
 
 
+MESH = pl.DeviceIdType.MESH
+NT = (((1,), (1,)), ((), ()))
+wire = jnp.float32
+
+
+def piece_plan(shard_rows, high):
+    piece = -(-shard_rows // (16 * high)) * 16
+    step = (shard_rows - piece) // (high - 1)
+    return (piece, step)
+
+
+def kernel_fits(rows, depth, width, shard_rows, blk_count, group_count):
+    if blk_count % 2 or group_count % 4 or blk_count < 4 or shard_rows % 16 or rows % 128:
+        return False
+    if width % 256 or depth % 128:
+        return False
+    high = blk_count // 2
+    piece, step = piece_plan(shard_rows, high)
+    return (shard_rows - piece) % (high - 1) == 0 and step % 16 == 0 and 0 <= step <= piece
+
+
+def step_kernel(
+    H, Z, chunks,
+    feat_ref, teach_ref, text_ref, ids_ref, w_ref, m1_ref, m2_ref,
+    loss_ref, first_ref, second_ref, out_ref,
+    tb, fb, fs, both, stu, pull, gbuf, gT, pf, pb, zr, hgb, wbuf,
+    ssem, rsem,
+):
+    rows, depth = text_ref.shape
+    width = feat_ref.shape[1]
+    half = width // 2
+    shard = m1_ref.shape[0]
+    piece, pstep = piece_plan(shard, H)
+    groups = 2 * Z
+    bi = lax.axis_index("blk")
+    gi = lax.axis_index("group")
+    h, c = bi // 2, bi % 2
+    z, x = gi // 2, gi % 2
+    oc, ox = 1 - c, 1 - x
+
+    def dev(z_, x_, h_, c_):
+        return (h_ * 2 + c_, z_ * 2 + x_)
+
+    sib = dev(z, x, h, oc)
+    names = {}
+    pending = []
+
+    def copy(name, src, dst, to):
+        idx = names.setdefault(name, len(names))
+        return pltpu.make_async_remote_copy(
+            src_ref=src, dst_ref=dst, send_sem=ssem.at[idx], recv_sem=rsem.at[idx],
+            device_id=to, device_id_type=MESH,
+        )
+
+    def send(name, src, dst, to):
+        op = copy(name, src, dst, to)
+        op.start()
+        pending.append(op)
+
+    def arrived(name, dst):
+        copy(name, dst, dst, sib).wait_recv()
+
+    peers = [sib, dev(z, ox, h, c)]
+    for j in range(1, H):
+        peers += [dev(z, x, (h + j) % H, c), dev(z, ox, (h + j) % H, c)]
+    for k in range(1, Z):
+        peers.append(dev((z + k) % Z, x, h, c))
+    barrier = pltpu.get_barrier_semaphore()
+    for peer in peers:
+        pl.semaphore_signal(barrier, inc=1, device_id=peer, device_id_type=MESH)
+
+    t32 = text_ref[...].astype(jnp.float32)
+    tb[0] = (t32 * lax.rsqrt(jnp.sum(t32 * t32, axis=-1, keepdims=True) + norm_eps)).astype(jnp.bfloat16)
+    fb[0] = feat_ref[...]
+    pl.semaphore_wait(barrier, len(peers))
+
+    far = 2 * H
+    chunk = rows // chunks
+    parts = [pl.ds(i * chunk, chunk) for i in range(chunks)]
+    for i, p in enumerate(parts):
+        send(("F", 0, i), tb.at[0, p], tb.at[far, p], dev((z + Z // 2) % Z, x, h, c))
+    for j in range(1, H):
+        send(("O", j), tb.at[0], tb.at[2 * j], dev(z, x, (h + H - j) % H, c))
+    send(("Os", 0), tb.at[0], tb.at[1], sib)
+    send(("fx", 0), fb.at[0], fb.at[H], dev(z, ox, h, c))
+    for j in range(1, H):
+        send(("fy", j), fb.at[0], fb.at[j], dev(z, x, (h + H - j) % H, c))
+
+    def my_half(col):
+        return pl.ds(pl.multiple_of(col * half, 128), half)
+
+    def feature_slot(s):
+        fs[pl.ds(2 * s * rows, rows), :] = fb[s, :, my_half(c)]
+        send(("fs", s), fb.at[s, :, my_half(oc)], fs.at[pl.ds((2 * s + 1) * rows, rows), :], sib)
+
+    feature_slot(0)
+
+    projected = lax.dot_general(feat_ref[...], w_ref[...], NT, preferred_element_type=jnp.float32)
+    inverse = lax.rsqrt(jnp.sum(projected * projected, axis=-1, keepdims=True) + norm_eps)
+    student = projected * inverse
+    stu[...] = student
+    both[0:rows] = student.astype(jnp.bfloat16)
+    e32 = teach_ref[...].astype(jnp.float32)
+    both[rows : 2 * rows] = (
+        e32 * lax.rsqrt(jnp.sum(e32 * e32, axis=-1, keepdims=True) + norm_eps)
+    ).astype(jnp.bfloat16)
+
+    def ids_row(b_, g_):
+        return ids_ref[pl.ds(b_ * groups + g_, 1), :]
+
+    left = jnp.transpose(jnp.broadcast_to(ids_row(bi, gi).astype(jnp.float32), (rows, rows)))[:, 0:1]
+    partner = (gi + Z) % groups
+    total = [jnp.zeros((rows, 1), jnp.float32)]
+
+    def pair_step(is_far, dh):
+        slot = is_far * far + 2 * dh
+        texts = tb[slot : slot + 2].reshape(2 * rows, depth)
+        g_ = partner if is_far else gi
+        h_ = (h + dh) % H
+        right = jnp.concatenate([ids_row(h_ * 2 + c, g_), ids_row(h_ * 2 + oc, g_)], axis=1)
+        logits = lax.dot_general(both[...], texts, NT, preferred_element_type=jnp.float32)
+        s_logit = student_scale * logits[0:rows] + student_bias
+        t_logit = teacher_scale * logits[rows : 2 * rows] + teacher_bias
+        labels = (left == right.astype(jnp.float32)).astype(jnp.float32)
+        target = (1.0 - label_mix) * labels + label_mix * jax.nn.sigmoid(t_logit)
+        small = jnp.exp(-jnp.abs(s_logit))
+        soft = jnp.maximum(s_logit, 0.0) + jnp.log1p(small)
+        total[0] = total[0] + jnp.sum(soft - target * s_logit, axis=1, keepdims=True)
+        coeff = (jax.nn.sigmoid(s_logit) - target).astype(jnp.bfloat16)
+        pulled = jnp.dot(coeff, texts, preferred_element_type=jnp.float32)
+        if slot == 0:
+            pull[...] = pulled
+        else:
+            pull[...] += pulled
+
+    def forward_far(i):
+        p = parts[i]
+        arrived(("F", 0, i), tb.at[far, p])
+        for j in range(1, H):
+            send(("F", j, i), tb.at[far, p], tb.at[far + 2 * j, p], dev(z, x, (h + H - j) % H, c))
+        send(("Fs", 0, i), tb.at[far, p], tb.at[far + 1, p], sib)
+
+    def forward_side(i):
+        p = parts[i]
+        for j in range(1, H):
+            arrived(("F", j, i), tb.at[far + 2 * j, p])
+            send(("Fs", j, i), tb.at[far + 2 * j, p], tb.at[far + 2 * j + 1, p], sib)
+
+    arrived(("Os", 0), tb.at[1])
+    pair_step(0, 0)
+    for i in range(chunks):
+        forward_far(i)
+        if i == 0:
+            for j in range(1, H):
+                arrived(("O", j), tb.at[2 * j])
+                send(("Os", j), tb.at[2 * j], tb.at[2 * j + 1], sib)
+        if i > 0:
+            forward_side(i - 1)
+        if i == chunks // 2:
+            for j in range(1, H):
+                arrived(("fy", j), fb.at[j])
+                send(("fx", j), fb.at[j], fb.at[H + j], dev(z, ox, h, c))
+                feature_slot(j)
+            arrived(("fx", 0), fb.at[H])
+            feature_slot(H)
+    for j in range(1, H):
+        arrived(("Os", j), tb.at[2 * j + 1])
+        pair_step(0, j)
+    forward_side(chunks - 1)
+    for i in range(chunks):
+        arrived(("Fs", 0, i), tb.at[far + 1, parts[i]])
+    pair_step(1, 0)
+    for j in range(1, H):
+        for i in range(chunks):
+            arrived(("Fs", j, i), tb.at[far + 2 * j + 1, parts[i]])
+        pair_step(1, j)
+
+    loss_ref[...] = jnp.transpose(jnp.broadcast_to(total[0], (rows, rows)))[0:1] / rows
+    gs = (student_scale / rows) * pull[...]
+    st = stu[...]
+    grad = (inverse * (gs - st * jnp.sum(st * gs, axis=-1, keepdims=True))).astype(jnp.bfloat16)
+    gbuf[...] = jnp.transpose(grad.astype(jnp.float32)).astype(jnp.bfloat16).reshape(gbuf.shape)
+
+    def offset(h_):
+        return pl.multiple_of(h_ * pstep, 16)
+
+    def lanes(s):
+        return pl.ds(s * rows, rows)
+
+    gT[:, :, lanes(0)] = gbuf[:, x, pl.ds(offset(h), piece), :]
+    for ex in (1, 0):
+        for eh in range(H):
+            if ex or eh:
+                x_, h_ = (x + ex) % 2, (h + H - eh) % H
+                s = ex * H + eh
+                send(
+                    ("g", s), gbuf.at[:, x_, pl.ds(offset(h_), piece), :], gT.at[:, :, lanes(2 * s)],
+                    dev(z, x_, h_, c),
+                )
+    send(("gs", 0), gT.at[:, :, lanes(0)], gT.at[:, :, lanes(1)], sib)
+    for j in range(1, H):
+        arrived(("fx", j), fb.at[H + j])
+        feature_slot(H + j)
+    for s in range(1, 2 * H):
+        arrived(("g", s), gT.at[:, :, lanes(2 * s)])
+        send(("gs", s), gT.at[:, :, lanes(2 * s)], gT.at[:, :, lanes(2 * s + 1)], sib)
+    for s in range(2 * H):
+        arrived(("fs", s), fs.at[pl.ds((2 * s + 1) * rows, rows), :])
+    for s in range(2 * H):
+        arrived(("gs", s), gT.at[:, :, lanes(2 * s + 1)])
+
+    summed = jnp.dot(
+        gT[...].reshape(Z * piece, 4 * H * rows), fs[...], preferred_element_type=jnp.float32
+    ).reshape(Z, piece, half)
+    pf[...] = summed
+    pb[...] = summed.astype(pb.dtype)
+    order = sorted(range(1, Z), key=lambda k: -min(k, Z - k))
+    for k in order:
+        send(("z", k), pb.at[(z + Z - k) % Z], zr.at[k - 1], dev((z + Z - k) % Z, x, h, c))
+    hg = pf[z]
+    for k in reversed(order):
+        arrived(("z", k), zr.at[k - 1])
+        hg = hg + zr[k - 1].astype(jnp.float32)
+    hgb[0] = hg
+
+    def moments(m1, m2, g):
+        return (
+            beta_one * m1 + (1.0 - beta_one) * g,
+            beta_two * m2 + (1.0 - beta_two) * g * g,
+        )
+
+    mine = (pl.ds(offset(h), piece), my_half(c))
+    first, second = moments(m1_ref[mine], m2_ref[mine], hg)
+    own = w_ref[
+        pl.ds(pl.multiple_of(gi * shard + h * pstep, 16), piece), my_half(c)
+    ].astype(jnp.float32)
+    first_hat = first / (1.0 - beta_one**adam_step)
+    second_hat = second / (1.0 - beta_two**adam_step)
+    updated = own - learn_rate * (first_hat / (jnp.sqrt(second_hat) + adam_eps) + weight_decay * own)
+    wbuf[z, x, h, c] = updated.astype(jnp.bfloat16)
+
+    def wslot(k, x_, h_, c_):
+        return wbuf.at[(z + k) % Z, x_, h_, c_]
+
+    for k in order:
+        send(("wz", k), wslot(0, x, h, c), wslot(0, x, h, c), dev((z + Z - k) % Z, x, h, c))
+
+    def spread(k):
+        mine_k = wslot(k, x, h, c)
+        send(("wx", k, 0), mine_k, mine_k, dev(z, ox, h, c))
+        for j in range(1, H):
+            send(("wy", k, j), mine_k, mine_k, dev(z, x, (h + H - j) % H, c))
+        send(("ws", k, 0, 0), mine_k, mine_k, sib)
+
+    spread(0)
+    for j in range(1, H):
+        send(("h", j), hgb.at[0], hgb.at[2 * j], dev(z, x, (h + H - j) % H, c))
+    send(("hs", 0), hgb.at[0], hgb.at[1], sib)
+
+    def relay(k):
+        over_x = wslot(k, ox, h, c)
+        arrived(("wx", k, 0), over_x)
+        if k % 2 == 0:
+            for j in range(1, H):
+                send(("wd", k, j), over_x, over_x, dev(z, x, (h + H - j) % H, c))
+        send(("ws", k, 1, 0), over_x, over_x, sib)
+        for j in range(1, H):
+            over_y = wslot(k, x, (h + j) % H, c)
+            arrived(("wy", k, j), over_y)
+            if k % 2 == 1:
+                send(("wd", k, j), over_y, over_y, dev(z, ox, h, c))
+            send(("ws", k, 0, j), over_y, over_y, sib)
+
+    near = [0] + list(reversed(order))
+    for n, k in enumerate(near[1:]):
+        arrived(("wz", k), wslot(k, x, h, c))
+        spread(k)
+        relay(near[n])
+        if n == 0:
+            for j in range(1, H):
+                arrived(("h", j), hgb.at[2 * j])
+                send(("hs", j), hgb.at[2 * j], hgb.at[2 * j + 1], sib)
+    relay(near[-1])
+    for k in near:
+        for j in range(1, H):
+            diag = wslot(k, ox, (h + j) % H, c)
+            arrived(("wd", k, j), diag)
+            send(("ws", k, 1, j), diag, diag, sib)
+
+    for j in range(H):
+        arrived(("hs", j), hgb.at[2 * j + 1])
+    for h_ in reversed(range(H)):
+        for c_ in range(2):
+            at = (pl.ds(h_ * pstep, piece), pl.ds(c_ * half, half))
+            slot = (h_ - h + H) % H * 2 + (c_ + c) % 2
+            first_ref[at], second_ref[at] = moments(m1_ref[at], m2_ref[at], hgb[slot])
+
+    for k in near:
+        for ex in range(2):
+            for j in range(H):
+                arrived(("ws", k, ex, j), wslot(k, ox if ex else x, (h + j) % H, oc))
+    for z_ in range(Z):
+        for x_ in range(2):
+            for h_ in reversed(range(H)):
+                for c_ in range(2):
+                    at = (pl.ds((z_ * 2 + x_) * shard + h_ * pstep, piece), pl.ds(c_ * half, half))
+                    out_ref[at] = wbuf[z_, x_, h_, c_]
+    for op in pending:
+        op.wait_send()
+
+
+def step_per_device(
+    student_features, teacher_image, text_embeds, pair_ids, head_weights, moment_first, moment_second
+):
+    rows, width = student_features.shape
+    depth = head_weights.shape[0]
+    shard = moment_first.shape[0]
+    blk_count = lax.axis_size("blk")
+    group_count = lax.axis_size("group")
+    args = (student_features, teacher_image, text_embeds, pair_ids, head_weights, moment_first, moment_second)
+    if not kernel_fits(rows, depth, width, shard, blk_count, group_count):
+        return per_device(*args)
+    H, Z = blk_count // 2, group_count // 2
+    chunks = max(1, rows // 32)
+    piece, _ = piece_plan(shard, H)
+    half = width // 2
+    bf16, f32 = jnp.bfloat16, jnp.float32
+    sems = 8 + 3 * H * (chunks + 4) + 10 * H * Z + 4 * Z
+    vmem = pl.BlockSpec(memory_space=pltpu.VMEM)
+    losses, new_first, new_second, new_weights = pl.pallas_call(
+        functools.partial(step_kernel, H, Z, chunks),
+        out_shape=(
+            jax.ShapeDtypeStruct((1, rows), f32),
+            jax.ShapeDtypeStruct(moment_first.shape, f32),
+            jax.ShapeDtypeStruct(moment_second.shape, f32),
+            jax.ShapeDtypeStruct(head_weights.shape, bf16),
+        ),
+        in_specs=[vmem] * 7,
+        out_specs=(vmem,) * 4,
+        scratch_shapes=[
+            pltpu.VMEM((4 * H, rows, depth), bf16),
+            pltpu.VMEM((2 * H, rows, width), bf16),
+            pltpu.VMEM((4 * H * rows, half), bf16),
+            pltpu.VMEM((2 * rows, depth), bf16),
+            pltpu.VMEM((rows, depth), f32),
+            pltpu.VMEM((rows, depth), f32),
+            pltpu.VMEM((Z, 2, shard, rows), bf16),
+            pltpu.VMEM((Z, piece, 4 * H * rows), bf16),
+            pltpu.VMEM((Z, piece, half), f32),
+            pltpu.VMEM((Z, piece, half), wire),
+            pltpu.VMEM((Z - 1, piece, half), wire),
+            pltpu.VMEM((2 * H, piece, half), f32),
+            pltpu.VMEM((Z, 2, H, 2, piece, half), bf16),
+            pltpu.SemaphoreType.DMA((sems,)),
+            pltpu.SemaphoreType.DMA((sems,)),
+        ],
+        compiler_params=pltpu.CompilerParams(
+            collective_id=0, has_side_effects=True, vmem_limit_bytes=40 * 1024 * 1024
+        ),
+    )(
+        student_features, teacher_image, text_embeds, pair_ids.reshape(-1, rows),
+        head_weights, moment_first, moment_second,
+    )
+    return (losses.reshape(rows), new_first, new_second, new_weights)
+
+
 def solution(mesh):
     placed = (
         P(("blk", "group"), None),
@@ -129,7 +499,7 @@
         P("group", None),
     )
     return jax.shard_map(
-        per_device,
+        step_per_device,
         mesh=mesh,
         in_specs=placed,
         out_specs=(P(("blk", "group")), P("group", None), P("group", None), P()),

time: 233 us -> 77.9 us (0.33)
  waiting for transfers between devices: 197 us -> 0 us
  Pallas kernels: 0 us -> 66.2 us
  between operations: 13.9 us -> 0.66 us
  matrix products: 7.89 us -> 0 us
  other arithmetic: 6.1 us -> 0 us
  local copies, waits for them, and re-layouts: 4.32 us -> 10.3 us
  starting transfers between devices: 4.26 us -> 0 us
    reduce_scatter x1 -> x0, waiting for transfers between devices: 79.3 us -> none  [per_device(): lax.psum_scatter(lax.dot_general(grad_projected, student_features, (((0,)...]
    all_gather x2 -> x0, waiting for transfers between devices: 69.1 us -> none  [the longest x1 46.3 us: per_device(): lax.all_gather(updated.astype(jnp.bfloat16), 'group', axis=0, tiled=True)]
    pallas_call x0 -> x1, Pallas kernels: none -> 66.2 us  [step_per_device(): pl.pallas_call(functools.partial(step_kernel, H, Z, chunks), out_shape=(j...]
    psum x1 -> x0, waiting for transfers between devices: 34.7 us -> none  [per_device(): head_grad = lax.psum(group_grad, 'blk')]
    ppermute x1 -> x0, waiting for transfers between devices: 13.3 us -> none  [from_partner(): lax.ppermute(shard, axis, [(i, i ^ 1 << bit) for i in range(lax.axis_size...]
    dot_general x5 -> x0, matrix products: 7.89 us -> none  [the longest x1 2.76 us: pair_terms(): lax.dot_general(teacher_rows, text_rows, dims, preferred_element_type=jnp...]
    unnamed x13 -> x18, local copies, waits for them, and re-layouts: 2.82 us -> 10.3 us
    ppermute x1 -> x0, starting transfers between devices: 4.1 us -> none  [from_partner(): lax.ppermute(shard, axis, [(i, i ^ 1 << bit) for i in range(lax.axis_size...]
  transfers between devices with their start and end apart: 5 -> 0, of which waited for: 5 -> 0; matrix products, arithmetic and copies ran while one was open for 1% -> 0% of each run, Pallas kernels for 0% -> 0%
where the time goes in v1:
time: 77.9 us; the launch traced here: 77.2 us
  Pallas kernels  66.2 us (85%)
  local copies, waits for them, and re-layouts  10.3 us (13%)
    pallas_call x1, Pallas kernels, step_per_device(): pl.pallas_call(functools.partial(step_kernel, H, Z, chunks), out_shape=(j...  66.2 us
    unnamed x18, local copies, waits for them, and re-layouts  10.3 us

profile of v1, /device:TPU:0, one launch (start us, length us, event | category | flops | bytes accessed | tf_op | source)
XLA Modules:
  0.0 77.2 jit_solution(11877453236738801755)
XLA Ops:
  0.6 0.0 copy-start
  0.6 1.5 %copy-done = bf16[1152,768]{1,0:T(8,128)(2,1)S(1)} copy-done((bf16[1152,768]{1,0:T(8,128)(2,1)S(1)}, bf16[1152,768]{1,0:T(8,128)(2,1)}, u32[]{:S(2)}) %copy-start) | copy-done | bytes 1769496
  2.1 0.0 copy-start.1
  2.1 1.0 %copy-done.1 = f32[144,768]{1,0:T(8,128)S(1)} copy-done((f32[144,768]{1,0:T(8,128)S(1)}, f32[144,768]{1,0:T(8,128)}, u32[]{:S(2)}) %copy-start.1) | copy-done | bytes 442392
  3.1 0.0 copy-start.2
  3.1 1.0 %copy-done.2 = f32[144,768]{1,0:T(8,128)S(1)} copy-done((f32[144,768]{1,0:T(8,128)S(1)}, f32[144,768]{1,0:T(8,128)}, u32[]{:S(2)}) %copy-start.2) | copy-done | bytes 442392
  4.1 0.0 copy-start.3
  4.1 1.0 %copy-done.3 = bf16[128,1152]{1,0:T(8,128)(2,1)S(1)} copy-done((bf16[128,1152]{1,0:T(8,128)(2,1)S(1)}, bf16[128,1152]{1,0:T(8,128)(2,1)}, u32[]{:S(2)}) %copy-start.3) | copy-done | bytes 294936
  5.1 0.0 copy-start.4
  5.1 1.0 %copy-done.4 = bf16[128,1152]{1,0:T(8,128)(2,1)S(1)} copy-done((bf16[128,1152]{1,0:T(8,128)(2,1)S(1)}, bf16[128,1152]{1,0:T(8,128)(2,1)}, u32[]{:S(2)}) %copy-start.4) | copy-done | bytes 294936
  6.1 0.0 copy-start.5
  6.1 0.9 %copy-done.5 = bf16[128,768]{1,0:T(8,128)(2,1)S(1)} copy-done((bf16[128,768]{1,0:T(8,128)(2,1)S(1)}, bf16[128,768]{1,0:T(8,128)(2,1)}, u32[]{:S(2)}) %copy-start.5) | copy-done | bytes 196632
  7.0 0.0 copy-start.6
  7.0 0.7 copy-done.6
  7.7 66.2 %shard_map.102 = (f32[1,128]{1,0:T(1,128)S(1)}, f32[144,768]{1,0:T(8,128)S(1)}, f32[144,768]{1,0:T(8,128)S(1)}, bf16[1152,768]{1,0:T(8,128)(2,1)S(1)}) custom-call(bf16[128,768]{1,0:T(8,128)(2,1)S(1)} %copy-done.5, bf16[128,1152]{1,0:T(8,128)(2,1)S(1)} %copy-done.3, bf16[128,1152]{1,0:T(8,128)(2,1)S(1)} %copy-done.4, s32[32,128]{1,0:T(8,128)S(1)} %bitcast.2, ...), custom_call_target="tpu_custom_call" | custom-call | tf_op jit(solution)/shard_map/pallas_call | solution.py:454
  73.9 0.5 copy.15
  74.4 0.8 copy.16
  75.2 0.8 copy.17
  76.0 1.2 %copy.18 = bf16[1152,768]{1,0:T(8,128)(2,1)} copy(bf16[1152,768]{1,0:T(8,128)(2,1)S(1)} %get-tuple-element.19) | data formatting | bytes 3538944
Async XLA Ops:
  0.6 1.5 %copy-start = (bf16[1152,768]{1,0:T(8,128)(2,1)S(1)}, bf16[1152,768]{1,0:T(8,128)(2,1)}, u32[]{:S(2)}) copy-start(bf16[1152,768]{1,0:T(8,128)(2,1)} %w_ref.1) | copy-start | bytes 5308420
  2.1 1.0 %copy-start.1 = (f32[144,768]{1,0:T(8,128)S(1)}, f32[144,768]{1,0:T(8,128)}, u32[]{:S(2)}) copy-start(f32[144,768]{1,0:T(8,128)} %m1_ref.1) | copy-start | bytes 1327108
  3.1 1.0 %copy-start.2 = (f32[144,768]{1,0:T(8,128)S(1)}, f32[144,768]{1,0:T(8,128)}, u32[]{:S(2)}) copy-start(f32[144,768]{1,0:T(8,128)} %m2_ref.1) | copy-start | bytes 1327108
  4.1 1.0 %copy-start.3 = (bf16[128,1152]{1,0:T(8,128)(2,1)S(1)}, bf16[128,1152]{1,0:T(8,128)(2,1)}, u32[]{:S(2)}) copy-start(bf16[128,1152]{1,0:T(8,128)(2,1)} %teach_ref.1) | copy-start | bytes 884740
  5.1 1.0 %copy-start.4 = (bf16[128,1152]{1,0:T(8,128)(2,1)S(1)}, bf16[128,1152]{1,0:T(8,128)(2,1)}, u32[]{:S(2)}) copy-start(bf16[128,1152]{1,0:T(8,128)(2,1)} %text_ref.1) | copy-start | bytes 884740
  6.1 0.9 %copy-start.5 = (bf16[128,768]{1,0:T(8,128)(2,1)S(1)}, bf16[128,768]{1,0:T(8,128)(2,1)}, u32[]{:S(2)}) copy-start(bf16[128,768]{1,0:T(8,128)(2,1)} %feat_ref.1) | copy-start | bytes 589828
  7.0 0.7 copy-start.6

commit v2 on v1

--- a/solution.py
+++ b/solution.py
@@ -124,7 +124,7 @@
 
 MESH = pl.DeviceIdType.MESH
 NT = (((1,), (1,)), ((), ()))
-wire = jnp.float32
+wire = jnp.bfloat16
 
 
 def piece_plan(shard_rows, high):
@@ -145,10 +145,12 @@
 
 def step_kernel(
     H, Z, chunks,
+    feat_hbm, teach_hbm, text_hbm, ids_hbm, w_hbm, m1_hbm, m2_hbm,
+    loss_hbm, first_hbm, second_hbm, out_hbm,
     feat_ref, teach_ref, text_ref, ids_ref, w_ref, m1_ref, m2_ref,
-    loss_ref, first_ref, second_ref, out_ref,
-    tb, fb, fs, both, stu, pull, gbuf, gT, pf, pb, zr, hgb, wbuf,
-    ssem, rsem,
+    tb, fb, fs, both, stu, pull, gbuf, gT, pf, pb, zr, hgb,
+    loss_ref, first_ref, second_ref, wbuf,
+    ssem, rsem, lsem,
 ):
     rows, depth = text_ref.shape
     width = feat_ref.shape[1]
@@ -184,6 +186,21 @@
     def arrived(name, dst):
         copy(name, dst, dst, sib).wait_recv()
 
+    loads = {}
+    for n, (name, src, dst) in enumerate((
+        ("text", text_hbm, text_ref), ("feat", feat_hbm, feat_ref), ("w", w_hbm, w_ref),
+        ("teach", teach_hbm, teach_ref), ("ids", ids_hbm, ids_ref), ("m1", m1_hbm, m1_ref), ("m2", m2_hbm, m2_ref),
+    )):
+        loads[name] = pltpu.make_async_copy(src, dst, lsem.at[n])
+        loads[name].start()
+
+    def store(src, dst):
+        op = pltpu.make_async_copy(src, dst, lsem.at[7 + len(stores)])
+        op.start()
+        stores.append(op)
+
+    stores = []
+
     peers = [sib, dev(z, ox, h, c)]
     for j in range(1, H):
         peers += [dev(z, x, (h + j) % H, c), dev(z, ox, (h + j) % H, c)]
@@ -193,8 +210,10 @@
     for peer in peers:
         pl.semaphore_signal(barrier, inc=1, device_id=peer, device_id_type=MESH)
 
+    loads["text"].wait()
     t32 = text_ref[...].astype(jnp.float32)
     tb[0] = (t32 * lax.rsqrt(jnp.sum(t32 * t32, axis=-1, keepdims=True) + norm_eps)).astype(jnp.bfloat16)
+    loads["feat"].wait()
     fb[0] = feat_ref[...]
     pl.semaphore_wait(barrier, len(peers))
 
@@ -207,8 +226,6 @@
         send(("O", j), tb.at[0], tb.at[2 * j], dev(z, x, (h + H - j) % H, c))
     send(("Os", 0), tb.at[0], tb.at[1], sib)
     send(("fx", 0), fb.at[0], fb.at[H], dev(z, ox, h, c))
-    for j in range(1, H):
-        send(("fy", j), fb.at[0], fb.at[j], dev(z, x, (h + H - j) % H, c))
 
     def my_half(col):
         return pl.ds(pl.multiple_of(col * half, 128), half)
@@ -219,11 +236,14 @@
 
     feature_slot(0)
 
+    loads["w"].wait()
     projected = lax.dot_general(feat_ref[...], w_ref[...], NT, preferred_element_type=jnp.float32)
     inverse = lax.rsqrt(jnp.sum(projected * projected, axis=-1, keepdims=True) + norm_eps)
     student = projected * inverse
     stu[...] = student
     both[0:rows] = student.astype(jnp.bfloat16)
+    for name in ("teach", "ids", "m1", "m2"):
+        loads[name].wait()
     e32 = teach_ref[...].astype(jnp.float32)
     both[rows : 2 * rows] = (
         e32 * lax.rsqrt(jnp.sum(e32 * e32, axis=-1, keepdims=True) + norm_eps)
@@ -282,24 +302,27 @@
             forward_side(i - 1)
         if i == chunks // 2:
             for j in range(1, H):
-                arrived(("fy", j), fb.at[j])
-                send(("fx", j), fb.at[j], fb.at[H + j], dev(z, ox, h, c))
-                feature_slot(j)
+                arrived(("Os", j), tb.at[2 * j + 1])
+                pair_step(0, j)
             arrived(("fx", 0), fb.at[H])
             feature_slot(H)
     for j in range(1, H):
-        arrived(("Os", j), tb.at[2 * j + 1])
-        pair_step(0, j)
+        send(("fy", j), fb.at[0], fb.at[j], dev(z, x, (h + H - j) % H, c))
     forward_side(chunks - 1)
     for i in range(chunks):
         arrived(("Fs", 0, i), tb.at[far + 1, parts[i]])
     pair_step(1, 0)
     for j in range(1, H):
+        arrived(("fy", j), fb.at[j])
+        send(("fx", j), fb.at[j], fb.at[H + j], dev(z, ox, h, c))
+        feature_slot(j)
+    for j in range(1, H):
         for i in range(chunks):
             arrived(("Fs", j, i), tb.at[far + 2 * j + 1, parts[i]])
         pair_step(1, j)
 
     loss_ref[...] = jnp.transpose(jnp.broadcast_to(total[0], (rows, rows)))[0:1] / rows
+    store(loss_ref, loss_hbm)
     gs = (student_scale / rows) * pull[...]
     st = stu[...]
     grad = (inverse * (gs - st * jnp.sum(st * gs, axis=-1, keepdims=True))).astype(jnp.bfloat16)
@@ -376,22 +399,22 @@
             send(("wy", k, j), mine_k, mine_k, dev(z, x, (h + H - j) % H, c))
         send(("ws", k, 0, 0), mine_k, mine_k, sib)
 
-    spread(0)
     for j in range(1, H):
         send(("h", j), hgb.at[0], hgb.at[2 * j], dev(z, x, (h + H - j) % H, c))
     send(("hs", 0), hgb.at[0], hgb.at[1], sib)
+    spread(0)
 
     def relay(k):
         over_x = wslot(k, ox, h, c)
         arrived(("wx", k, 0), over_x)
-        if k % 2 == 0:
+        if k == 0:
             for j in range(1, H):
                 send(("wd", k, j), over_x, over_x, dev(z, x, (h + H - j) % H, c))
         send(("ws", k, 1, 0), over_x, over_x, sib)
         for j in range(1, H):
             over_y = wslot(k, x, (h + j) % H, c)
             arrived(("wy", k, j), over_y)
-            if k % 2 == 1:
+            if k != 0:
                 send(("wd", k, j), over_y, over_y, dev(z, ox, h, c))
             send(("ws", k, 0, j), over_y, over_y, sib)
 
@@ -418,6 +441,8 @@
             at = (pl.ds(h_ * pstep, piece), pl.ds(c_ * half, half))
             slot = (h_ - h + H) % H * 2 + (c_ + c) % 2
             first_ref[at], second_ref[at] = moments(m1_ref[at], m2_ref[at], hgb[slot])
+    store(first_ref, first_hbm)
+    store(second_ref, second_hbm)
 
     for k in near:
         for ex in range(2):
@@ -425,12 +450,39 @@
                 arrived(("ws", k, ex, j), wslot(k, ox if ex else x, (h + j) % H, oc))
     for z_ in range(Z):
         for x_ in range(2):
-            for h_ in reversed(range(H)):
+            for h_ in range(H):
                 for c_ in range(2):
-                    at = (pl.ds((z_ * 2 + x_) * shard + h_ * pstep, piece), pl.ds(c_ * half, half))
-                    out_ref[at] = wbuf[z_, x_, h_, c_]
+                    skip = piece - pstep if h_ else 0
+                    row = (z_ * 2 + x_) * shard + h_ * pstep + skip
+                    store(
+                        wbuf.at[z_, x_, h_, c_, pl.ds(skip, piece - skip), :],
+                        out_hbm.at[pl.ds(row, piece - skip), pl.ds(c_ * half, half)],
+                    )
     for op in pending:
         op.wait_send()
+    for op in stores:
+        op.wait()
+
+
+def store_kernel(cuts, *refs):
+    sources, outs, held = refs[:4], refs[4:8], refs[8:12]
+    sem_in, sem_out = refs[12:]
+    moves = [(n, slice(None)) for n in range(3)]
+    part = sources[3].shape[0] // cuts
+    moves += [(3, pl.ds(n * part, part)) for n in range(cuts)]
+    loads = [
+        pltpu.make_async_copy(sources[n].at[at], held[n].at[at], sem_in.at[i]) for i, (n, at) in enumerate(moves)
+    ]
+    stores = [
+        pltpu.make_async_copy(held[n].at[at], outs[n].at[at], sem_out.at[i]) for i, (n, at) in enumerate(moves)
+    ]
+    for op in loads:
+        op.start()
+    for load, op in zip(loads, stores):
+        load.wait()
+        op.start()
+    for op in stores:
+        op.wait()
 
 
 def step_per_device(
@@ -450,18 +502,25 @@
     half = width // 2
     bf16, f32 = jnp.bfloat16, jnp.float32
     sems = 8 + 3 * H * (chunks + 4) + 10 * H * Z + 4 * Z
-    vmem = pl.BlockSpec(memory_space=pltpu.VMEM)
-    losses, new_first, new_second, new_weights = pl.pallas_call(
+    hbm = pl.BlockSpec(memory_space=pltpu.HBM)
+    operands = (
+        student_features, teacher_image, text_embeds, pair_ids.reshape(-1, rows),
+        head_weights, moment_first, moment_second,
+    )
+    cuts = 4 if depth % 64 == 0 else 1
+    big = 60 * 1024 * 1024
+    shapes = (
+        jax.ShapeDtypeStruct((1, rows), f32),
+        jax.ShapeDtypeStruct(moment_first.shape, f32),
+        jax.ShapeDtypeStruct(moment_second.shape, f32),
+        jax.ShapeDtypeStruct(head_weights.shape, bf16),
+    )
+    done = pl.pallas_call(
         functools.partial(step_kernel, H, Z, chunks),
-        out_shape=(
-            jax.ShapeDtypeStruct((1, rows), f32),
-            jax.ShapeDtypeStruct(moment_first.shape, f32),
-            jax.ShapeDtypeStruct(moment_second.shape, f32),
-            jax.ShapeDtypeStruct(head_weights.shape, bf16),
-        ),
-        in_specs=[vmem] * 7,
-        out_specs=(vmem,) * 4,
-        scratch_shapes=[
+        out_shape=shapes,
+        in_specs=[hbm] * 7,
+        out_specs=(hbm,) * 4,
+        scratch_shapes=[pltpu.VMEM(a.shape, a.dtype) for a in operands] + [
             pltpu.VMEM((4 * H, rows, depth), bf16),
             pltpu.VMEM((2 * H, rows, width), bf16),
             pltpu.VMEM((4 * H * rows, half), bf16),
@@ -474,17 +533,27 @@
             pltpu.VMEM((Z, piece, half), wire),
             pltpu.VMEM((Z - 1, piece, half), wire),
             pltpu.VMEM((2 * H, piece, half), f32),
+            pltpu.VMEM((1, rows), f32),
+            pltpu.VMEM(moment_first.shape, f32),
+            pltpu.VMEM(moment_second.shape, f32),
             pltpu.VMEM((Z, 2, H, 2, piece, half), bf16),
             pltpu.SemaphoreType.DMA((sems,)),
             pltpu.SemaphoreType.DMA((sems,)),
+            pltpu.SemaphoreType.DMA((10 + 4 * H * Z,)),
         ],
         compiler_params=pltpu.CompilerParams(
-            collective_id=0, has_side_effects=True, vmem_limit_bytes=40 * 1024 * 1024
+            collective_id=0, has_side_effects=True, vmem_limit_bytes=big
         ),
-    )(
-        student_features, teacher_image, text_embeds, pair_ids.reshape(-1, rows),
-        head_weights, moment_first, moment_second,
-    )
+    )(*operands)
+    losses, new_first, new_second, new_weights = pl.pallas_call(
+        functools.partial(store_kernel, cuts),
+        out_shape=shapes,
+        in_specs=[hbm] * 4,
+        out_specs=(hbm,) * 4,
+        scratch_shapes=[pltpu.VMEM(a.shape, a.dtype) for a in shapes]
+        + [pltpu.SemaphoreType.DMA((3 + cuts,))] * 2,
+        compiler_params=pltpu.CompilerParams(vmem_limit_bytes=big),
+    )(*done)
     return (losses.reshape(rows), new_first, new_second, new_weights)
 
 

time: 77.9 us -> 69.4 us (0.89)
  local copies, waits for them, and re-layouts: 10.3 us -> 0 us
  Pallas kernels: 66.2 us -> 68.2 us
    unnamed x18 -> x0, local copies, waits for them, and re-layouts: 10.3 us -> none
    pallas_call x1 -> x2, Pallas kernels: 66.2 us -> 68.2 us  [the longest x1 65.6 us: step_per_device(): pl.pallas_call(functools.partial(step_kernel, H, Z, chunks), out_shape=sh...]
where the time goes in v2:
time: 69.4 us; the launch traced here: 68.8 us
  Pallas kernels  68.2 us (98%)
    pallas_call x1, Pallas kernels, step_per_device(): pl.pallas_call(functools.partial(step_kernel, H, Z, chunks), out_shape=sh...  65.6 us
    pallas_call x1, Pallas kernels, step_per_device(): pl.pallas_call(functools.partial(store_kernel, cuts), out_shape=shapes, i...  2.63 us

profile of v2, /device:TPU:0, one launch (start us, length us, event | category | flops | bytes accessed | tf_op | source)
XLA Modules:
  0.0 68.8 jit_solution(11350406035459837752)
XLA Ops:
  0.6 65.6 %shard_map.102 = (f32[1,128]{1,0:T(1,128)}, f32[144,768]{1,0:T(8,128)}, f32[144,768]{1,0:T(8,128)}, bf16[1152,768]{1,0:T(8,128)(2,1)}) custom-call(bf16[128,768]{1,0:T(8,128)(2,1)} %feat_hbm.1, bf16[128,1152]{1,0:T(8,128)(2,1)} %teach_hbm.1, bf16[128,1152]{1,0:T(8,128)(2,1)} %text_hbm.1, s32[32,128]{1,0:T(8,128)} %bitcast.2, bf16[1152,768]{1,0:T(8,128)(2,1)} %w_hbm.1, ...), custom_call_target="tpu_custom_call" | custom-call | tf_op jit(solution)/shard_map/pallas_call | solution.py:518
  66.2 2.6 %shard_map.103 = (f32[1,128]{1,0:T(1,128)}, f32[144,768]{1,0:T(8,128)}, f32[144,768]{1,0:T(8,128)}, bf16[1152,768]{1,0:T(8,128)(2,1)}) custom-call(f32[1,128]{1,0:T(1,128)} %get-tuple-element.12.refs_0_, f32[144,768]{1,0:T(8,128)} %get-tuple-element.13.refs_1_, f32[144,768]{1,0:T(8,128)} %get-tuple-element.14.refs_2_, ...), custom_call_target="tpu_custom_call" | custom-call | tf_op jit(solution)/shard_map/pallas_call | solution.py:548
